TPU v7x, 256 devices: a whole 4x4x8 slice. The times are simulated.
256 devices in a mesh: seq: 32 (over z, x), exp: 8 (over y, core).
Axes of the slice: x: 4, y: 4, z: 8, core: 2. Of those that a mesh axis runs over, the one named last changes fastest.
Arguments:
- mixer_input: bfloat16 [2048, 8192], P('seq', 'exp'), may hold values from -6 to 6
- gate_input: bfloat16 [2048, 8192], P('seq', 'exp'), may hold values from -6 to 6
- conv_weight: bfloat16 [4, 8192], P(None, 'exp'), may hold values from -3 to 3
- conv_bias: float32 [8192], P('exp'), may hold values from -3 to 3
- rank_weight: bfloat16 [8192, 256], P('exp'), may hold values from -0.0625 to 0.0625
- state_weight: bfloat16 [8192, 32], P('exp'), may hold values from -0.03125 to 0.03125
- delta_weight: bfloat16 [256, 8192], P(None, 'exp'), may hold values from -0.375 to 0.375
- delta_bias: float32 [8192], P('exp'), may hold values from -1 to 1
- log_rates: float32 [16, 8192], P(None, 'exp'), may hold values from -10 to -1
- skip_gain: float32 [8192], P('exp'), may hold values from 0.5 to 1.5
- out_proj: bfloat16 [8192, 4096], P('exp', 'seq'), may hold values from -0.0625 to 0.0625
- residual: bfloat16 [2048, 4096], P(('seq', 'exp')), may hold values from -3 to 3
- norm_gain: float32 [4096], replicated, may hold values from 0.5 to 1.5
- router: float32 [4096, 8], replicated, may hold values from -0.09375 to 0.09375
- w_gate: bfloat16 [8, 4096, 14336], P('exp', None, 'seq'), may hold values from -0.09375 to 0.09375
- w_up: bfloat16 [8, 4096, 14336], P('exp', None, 'seq'), may hold values from -0.09375 to 0.09375
- w_down: bfloat16 [8, 14336, 4096], P('exp', 'seq'), may hold values from -0.09375 to 0.09375
- routes: int32 [2048, 2], P(('seq', 'exp')), may hold values from 0 to 7, all different within a row; in each aligned block of 8 rows (0 to 7, 8 to 15, ...) at most 4 rows name the same one
Outputs:
- layer_out: bfloat16 [2048, 4096], P(('seq', 'exp'))
- expert_mix: float32 [2048, 4096], P(('seq', 'exp'))
Inputs may be any that keep to these rules, and one draw needn't show every extreme that they name: `routes`: each row names two different experts; among the 8 rows of one device no expert is named more than 4 times, a bound that some block reaches there on some device.
All inputs are finite; a program needn't handle non-finite values.
Results may differ from a plain program's by a relative error of at most 0.024.
Values may be sent and summed in bfloat16 or wider, within the bound.
No kernel may reach another device: no remote copies, remote signals or barrier semaphores. Data moves between devices by JAX's collectives and lax.ppermute only.
A program may use at most 128 MiB of HBM per device.

v0:
```python
import jax
import jax.numpy as jnp
from jax import lax
from jax.sharding import PartitionSpec as P


def shifted(block, axis, distance):
    devices = range(lax.axis_size(axis))
    route = [(i - distance, i) for i in devices if i - distance in devices]
    return lax.ppermute(block, axis, route)


def entering(array, axis, combine, identity):
    count, index = (lax.axis_size(axis), lax.axis_index(axis))
    everything = jax.tree.map(lambda part: lax.all_gather(part, axis), array)
    start = jax.tree.map(
        lambda part, zero: jnp.broadcast_to(jnp.asarray(zero, part.dtype), part.shape),
        array,
        identity,
    )

    def hop(k, before):
        reached = k < index
        new = combine(before, jax.tree.map(lambda part: part[k], everything))
        return jax.tree.map(lambda a, b: jnp.where(reached, a, b), new, before)

    return lax.fori_loop(0, count, hop, start)


def combine_pair(earlier, following):
    return (earlier[0] * following[0], following[0] * earlier[1] + following[1])


def body(
    mixer_input,
    gate_input,
    conv_weight,
    conv_bias,
    rank_weight,
    state_weight,
    delta_weight,
    delta_bias,
    log_rates,
    skip_gain,
    out_proj,
    residual,
    norm_gain,
    router,
    w_gate,
    w_up,
    w_down,
    routes,
):
    taps = conv_weight.shape[0]
    block_rows = mixer_input.shape[0]
    rim_rows = shifted(mixer_input[block_rows - (taps - 1) :], "seq", 1)
    padded = jnp.concatenate([rim_rows, mixer_input], axis=0)
    conv_sum = jnp.zeros(mixer_input.shape, jnp.float32) + conv_bias[None, :]
    for offset in range(taps):
        conv_sum = conv_sum + conv_weight[offset].astype(jnp.float32)[None, :] * padded[
            offset : offset + block_rows
        ].astype(jnp.float32)
    conv_act = jax.nn.silu(conv_sum).astype(jnp.bfloat16)
    delta_part = jnp.dot(conv_act, rank_weight, preferred_element_type=jnp.float32)
    state_part = jnp.dot(conv_act, state_weight, preferred_element_type=jnp.float32)
    delta_sum, state_maps = lax.psum((delta_part, state_part), "exp")
    delta_low = delta_sum.astype(jnp.bfloat16)
    states = log_rates.shape[0]
    input_map = state_maps[:, :states]
    output_map = state_maps[:, states:]
    delta = jax.nn.softplus(
        jnp.dot(delta_low, delta_weight, preferred_element_type=jnp.float32) + delta_bias[None, :]
    )
    decay_rate = jnp.exp(log_rates)
    conv_float = conv_act.astype(jnp.float32)
    driven = (delta * conv_float)[:, None, :] * input_map[:, :, None]
    decays = jnp.exp(-delta[:, None, :] * decay_rate[None])
    passed = jnp.cumsum(delta, axis=0)
    total_dt = passed[-1]
    weights_left = jnp.exp(-(total_dt[None, :] - passed)[:, None, :] * decay_rate[None])
    transform = (jnp.exp(-total_dt[None, :] * decay_rate), jnp.sum(weights_left * driven, axis=0))
    incoming = entering(
        transform, "seq", combine_pair, (jnp.ones_like(decay_rate), jnp.zeros_like(decay_rate))
    )
    start_state = incoming[1]

    def advance(carried, inputs):
        decay_t, driven_t, output_t = inputs
        carried = decay_t * carried + driven_t
        return (carried, jnp.sum(output_t[:, None] * carried, axis=0))

    last_state, scan_out = lax.scan(advance, start_state, (decays, driven, output_map))
    scan_out = scan_out + skip_gain[None, :] * conv_float
    gated = (scan_out * jax.nn.silu(gate_input.astype(jnp.float32))).astype(jnp.bfloat16)
    tok_dev = residual.shape[0]
    partial_value = jnp.dot(
        gated,
        lax.all_gather(out_proj, "seq", axis=1, tiled=True),
        preferred_element_type=jnp.float32,
    )
    mamba_out = lax.psum_scatter(partial_value, "exp", scatter_dimension=0, tiled=True)
    hidden = residual.astype(jnp.float32) + mamba_out
    mean_square = jnp.mean(hidden * hidden, axis=1, keepdims=True)
    normed = (hidden * lax.rsqrt(mean_square + 1e-05) * norm_gain[None, :]).astype(jnp.bfloat16)
    logits = jnp.dot(normed.astype(jnp.float32), router, precision=lax.Precision.HIGHEST)
    experts = router.shape[1]
    expert_ids = jnp.arange(experts, dtype=jnp.int32)
    matches = (routes[:, :, None] == expert_ids[None, None, :]).astype(jnp.float32)
    chosen = jnp.sum(matches * logits[:, None, :], axis=2)
    route_weights = jax.nn.sigmoid(chosen - chosen[:, ::-1])
    capacity = max(2, 4 * tok_dev // experts)
    flat_ids = routes.reshape(-1)
    route_pos = jnp.arange(flat_ids.shape[0], dtype=jnp.int32)
    earlier_same = (flat_ids[:, None] == flat_ids[None, :]) & (
        route_pos[None, :] < route_pos[:, None]
    )
    slot_rank = jnp.sum(earlier_same.astype(jnp.int32), axis=1)
    slot_of = flat_ids * capacity + slot_rank
    slot_ids = jnp.arange(experts * capacity, dtype=jnp.int32)
    placing = (slot_ids[:, None] == slot_of[None, :]).astype(jnp.bfloat16)
    repeated = jnp.repeat(normed, 2, axis=0)
    outbound = jnp.dot(placing, repeated, preferred_element_type=jnp.float32).astype(jnp.bfloat16)
    arrived = lax.all_to_all(outbound, "exp", split_axis=0, concat_axis=0, tiled=True)
    gate_local = w_gate[0]
    up_local = w_up[0]
    down_local = w_down[0]
    shard_part = lax.all_gather(arrived, "seq", axis=0, tiled=True)
    gate_part = jnp.dot(shard_part, gate_local, preferred_element_type=jnp.float32)
    up_part = jnp.dot(shard_part, up_local, preferred_element_type=jnp.float32)
    activated = (jax.nn.silu(gate_part) * up_part).astype(jnp.bfloat16)
    expert_out = lax.psum_scatter(
        jnp.dot(activated, down_local, preferred_element_type=jnp.float32).astype(jnp.bfloat16),
        "seq",
        scatter_dimension=0,
        tiled=True,
    ).astype(jnp.float32)
    returned = lax.all_to_all(expert_out, "exp", split_axis=0, concat_axis=0, tiled=True)
    picked = jnp.take(returned, slot_of, axis=0)
    moe_sum = jnp.sum(picked.reshape(tok_dev, 2, -1) * route_weights[:, :, None], axis=1)
    return ((hidden + moe_sum).astype(jnp.bfloat16), moe_sum)


def solution(mesh):
    in_specs = (
        P("seq", "exp"),
        P("seq", "exp"),
        P(None, "exp"),
        P("exp"),
        P("exp", None),
        P("exp", None),
        P(None, "exp"),
        P("exp"),
        P(None, "exp"),
        P("exp"),
        P("exp", "seq"),
        P(("seq", "exp"), None),
        P(),
        P(),
        P("exp", None, "seq"),
        P("exp", None, "seq"),
        P("exp", "seq", None),
        P(("seq", "exp"), None),
    )
    out_specs = (P(("seq", "exp"), None), P(("seq", "exp"), None))
    return jax.shard_map(body, mesh=mesh, in_specs=in_specs, out_specs=out_specs, check_vma=False)
```

profile of v0, /device:TPU:1, one launch (start us, length us, event | category | flops | bytes accessed | tf_op | source)
XLA Modules:
  0.0 738.1 jit_solution(16103797339628601987)
XLA Ops:
  8.0 3.9 collective-permute-start
  12.8 1.4 multiply_convert_fusion.1
  14.2 1.2 fusion.34
  15.4 1.0 fusion.35
  16.4 23.9 %all-reduce = (bf16[64,256]{1,0:T(8,128)(2,1)S(1)}, f32[64,32]{0,1:T(8,128)S(1)}) all-reduce(f32[64,256]{1,0:T(8,128)S(1)} %fusion.34, f32[64,32]{0,1:T(8,128)S(1)} %fusion.35), channel_id=1, replica_groups=mesh['seq'=32,'exp'=8] {'exp'}, use_global_device_ids=true, to_apply=%region_0.1 | all-reduce | flops 18432 | bytes 114688 | tf_op jit(solution)/shard_map/psum | solution.py:66
  40.3 1.0 fusion.30
  41.7 1.5 fusion.32
  43.2 4.3 broadcast_multiply_fusion
  49.2 77.0 %all-gather.13.cloned.1.call-done = f32[512,1024]{1,0:T(8,128)} async-done(((f32[16,1024]{1,0:T(8,128)}), f32[512,1024]{1,0:T(8,128)}) %all-gather.13.cloned.1.call-update) | async-done | bytes 2097168 | tf_op jit(solution)/shard_map/all_gather | solution.py:15
  126.2 78.3 %all-gather.11.cloned.1.call-done = f32[512,1024]{1,0:T(8,128)} async-done(((f32[16,1024]{1,0:T(8,128)}), f32[512,1024]{1,0:T(8,128)}) %all-gather.11.cloned.1.call-update) | async-done | bytes 2097168 | tf_op jit(solution)/shard_map/all_gather | solution.py:15
  204.5 30.0 %while.29 = (s32[]{:T(128)}, f32[16,1024]{1,0:T(8,128)S(1)}, s32[]{:T(128)}, f32[32,16,1024]{2,1,0:T(8,128)}, f32[32,16,1024]{2,1,0:T(8,128)}) while((s32[]{:T(128)}, f32[16,1024]{1,0:T(8,128)S(1)}, s32[]{:T(128)}, f32[32,16,1024]{2,1,0:T(8,128)}, f32[32,16,1024]{2,1,0:T(8,128)}) %tuple.91), condition=%wide.region_5.6_spmd.clone.clone, body=%wide.region_4.5_spmd.clone.sunk.clone | while | flops 65540 | bytes 262229 | solution.py:27
  234.5 71.4 %while.28 = (s32[]{:T(128)}, f32[16,1024]{1,0:T(8,128)S(1)}, f32[64,1024]{1,0:T(8,128)S(1)}, f32[64,16,1024]{2,1,0:T(8,128)}, f32[64,16,1024]{2,1,0:T(8,128)}, /*index=5*/f32[64,16]{1,0:T(8,128)S(1)}) while((s32[]{:T(128)}, f32[16,1024]{1,0:T(8,128)S(1)}, f32[64,1024]{1,0:T(8,128)S(1)}, f32[64,16,1024]{2,1,0:T(8,128)}, ...), condition=%wide.region_8.9_spmd.clone, body=%wide.region_6.8_spmd.sunk.clone | while | flops 64514 | bytes 274705 | solution.py:92
  237.9 1.0 multiply_reduce_fusion.6
  241.2 1.0 multiply_reduce_fusion.6
  260.2 1.0 multiply_reduce_fusion.6
  261.3 1.0 multiply_reduce_fusion.6
  262.4 1.0 multiply_reduce_fusion.6
  263.5 1.0 multiply_reduce_fusion.6
  264.7 1.0 multiply_reduce_fusion.6
  270.2 1.0 multiply_reduce_fusion.6
  271.4 1.0 multiply_reduce_fusion.6
  274.7 1.0 multiply_reduce_fusion.6
  275.8 1.0 multiply_reduce_fusion.6
  276.9 1.0 multiply_reduce_fusion.6
  278.1 1.0 multiply_reduce_fusion.6
  279.2 1.0 multiply_reduce_fusion.6
  284.8 1.0 multiply_reduce_fusion.6
  287.0 1.0 multiply_reduce_fusion.6
  288.1 1.0 multiply_reduce_fusion.6
  289.2 1.0 multiply_reduce_fusion.6
  290.4 1.0 multiply_reduce_fusion.6
  291.5 1.0 multiply_reduce_fusion.6
  292.6 1.0 multiply_reduce_fusion.6
  293.7 1.0 multiply_reduce_fusion.6
  298.2 1.0 multiply_reduce_fusion.6
  306.0 3.2 all-gather.7.cloned.1.call-done
  309.2 6.1 fusion.20
  315.7 32.0 %reduce-scatter.3.cloned.1.call-done = f32[8,4096]{1,0:T(8,128)} async-done(((f32[64,4096]{1,0:T(8,128)}), f32[8,4096]{1,0:T(8,128)}) %reduce-scatter.3.cloned.1.call-update) | async-done | bytes 131088 | tf_op jit(solution)/shard_map/reduce_scatter | solution.py:101
  347.7 1.1 multiply_reduce_fusion.3
  348.8 1.0 multiply_convert_fusion.2
  350.2 12.0 %all_to_all.28 = bf16[8,4,4096]{2,1,0:T(4,128)(2,1)S(1)} all-to-all(bf16[8,4,4096]{2,1,0:T(4,128)(2,1)S(1)} %all_to_all.18), channel_id=1, replica_groups=mesh['seq'=32,'exp'=8] {'exp'}, dimensions={0} | all-to-all | bytes 524288 | tf_op jit(solution)/shard_map/all_to_all | solution.py:123
  363.3 97.7 %all-gather.9.cloned.1.call-done = bf16[1024,4096]{1,0:T(8,128)(2,1)} async-done(((bf16[32,4096]{1,0:T(8,128)(2,1)}), bf16[1024,4096]{1,0:T(8,128)(2,1)}) %all-gather.9.cloned.1.call-update) | async-done | bytes 8388624 | tf_op jit(solution)/shard_map/all_gather | solution.py:127
  460.9 9.7 %fusion.5 = f32[1024,448]{0,1:T(8,128)} fusion(bf16[1024,4096]{1,0:T(8,128)(2,1)} %all-gather.9.cloned.1.call-done, bf16[1,4096,448]{1,2,0:T(8,128)(2,1)} %param.36), kind=kOutput, calls=%fused_computation.16 | convolution fusion | flops 3758096384 | bytes 13893632 | tf_op jit(solution)/shard_map/dot_general | solution.py:128
  470.6 15.4 %convolution_convert_fusion = bf16[1024,4096]{1,0:T(8,128)(2,1)} fusion(bf16[1,448,4096]{2,1,0:T(8,128)(2,1)} %param.38, f32[1024,448]{0,1:T(8,128)} %fusion.5, bf16[1024,4096]{1,0:T(8,128)(2,1)} %all-gather.9.cloned.1.call-done, bf16[1,4096,448]{1,2,0:T(8,128)(2,1)} %param.37), kind=kOutput, calls=%fused_computation.9 | convolution fusion | flops 7523139584 | bytes 25952256 | tf_op jit(solution)/shard_map/dot_general | solution.py:132
  486.3 222.6 %reduce-scatter.5.cloned.1.call-done = bf16[32,4096]{1,0:T(8,128)(2,1)} async-done(((bf16[1024,4096]{1,0:T(8,128)(2,1)}), bf16[32,4096]{1,0:T(8,128)(2,1)}) %reduce-scatter.5.cloned.1.call-update) | async-done | bytes 262160 | tf_op jit(solution)/shard_map/reduce_scatter | solution.py:131
  708.9 1.9 reshape.112
  710.8 8.9 %all-to-all-start.1 = ((f32[8,4,4096]{2,1,0:T(4,128)}), f32[8,4,4096]{2,1,0:T(4,128)S(1)}, u32[]{:S(2)}, u32[]{:S(2)}) async-start(f32[8,4,4096]{2,1,0:T(4,128)} %reshape.112), calls=%async_computation.3 | async-start | bytes 1048576 | tf_op jit(solution)/shard_map/all_to_all | solution.py:137
  720.2 9.0 %all-to-all-done.1 = f32[8,4,4096]{2,1,0:T(4,128)S(1)} async-done(((f32[8,4,4096]{2,1,0:T(4,128)}), f32[8,4,4096]{2,1,0:T(4,128)S(1)}, u32[]{:S(2)}, u32[]{:S(2)}) %all-to-all-start.1) | async-done | bytes 524320 | tf_op jit(solution)/shard_map/all_to_all | solution.py:137
  (268 shorter events, 84.8 us)
Async XLA Ops:
  7.2 33.1 %copy-start = (bf16[256,1024]{1,0:T(8,128)(2,1)S(1)}, bf16[256,1024]{1,0:T(8,128)(2,1)}, u32[]{:S(2)}) copy-start(bf16[256,1024]{1,0:T(8,128)(2,1)} %param.28) | copy-start | bytes 1572868
  7.2 119.0 %all-gather.13.cloned.1.call-start = ((), (), s32[]{:S(2)}) async-start(), calls=%async_computation.9 | async-start | bytes 2162688 | tf_op jit(solution)/shard_map/all_gather | solution.py:15
  8.0 4.8 collective-permute-start
  43.2 265.9 %copy-start.4 = (bf16[64,1024]{1,0:T(8,128)(2,1)S(1)}, bf16[64,1024]{1,0:T(8,128)(2,1)}, u32[]{:S(2)}) copy-start(bf16[64,1024]{1,0:T(8,128)(2,1)} %param.23) | copy-start | bytes 393220
  43.2 265.9 %copy-start.6 = (f32[1024]{0:T(1024)S(1)}, f32[1024]{0:T(1024)}, u32[]{:S(2)}) copy-start(f32[1024]{0:T(1024)} %param.31) | copy-start | bytes 12292
  47.6 157.0 %all-gather.11.cloned.1.call-start = ((), (), s32[]{:S(2)}) async-start(), calls=%async_computation.8 | async-start | bytes 2162688 | tf_op jit(solution)/shard_map/all_gather | solution.py:15
  48.3 260.9 %all-gather.7.cloned.1.call-start = ((), (), s32[]{:S(2)}) async-start(), calls=%async_computation.4 | async-start | bytes 8650752 | tf_op jit(solution)/shard_map/all_gather | solution.py:98
  49.0 298.7 %reduce-scatter.3.cloned.1.call-start = ((), (), s32[]{:S(2)}) async-start(), calls=%async_computation.5 | async-start | bytes 1179648 | tf_op jit(solution)/shard_map/reduce_scatter | solution.py:101
  309.2 6.2 copy-start.8
  309.2 38.5 %copy-start.2 = (bf16[8,4096]{1,0:T(8,128)(2,1)S(1)}, bf16[8,4096]{1,0:T(8,128)(2,1)}, u32[]{:S(2)}) copy-start(bf16[8,4096]{1,0:T(8,128)(2,1)} %param.33) | copy-start | bytes 196612
  309.2 39.6 %copy-start.7 = (f32[4096]{0:T(1024)S(1)}, f32[4096]{0:T(1024)}, u32[]{:S(2)}) copy-start(f32[4096]{0:T(1024)} %param.34) | copy-start | bytes 49156
  315.3 145.7 %all-gather.9.cloned.1.call-start = ((), (), s32[]{:S(2)}) async-start(), calls=%async_computation.6 | async-start | bytes 8650752 | tf_op jit(solution)/shard_map/all_gather | solution.py:127
  363.1 345.9 %reduce-scatter.5.cloned.1.call-start = ((), (), s32[]{:S(2)}) async-start(), calls=%async_computation.7 | async-start | bytes 8650752 | tf_op jit(solution)/shard_map/reduce_scatter | solution.py:131
  486.0 233.6 %copy-start.5 = (f32[4096,8]{0,1:T(8,128)S(1)}, f32[4096,8]{0,1:T(8,128)}, u32[]{:S(2)}) copy-start(f32[4096,8]{0,1:T(8,128)} %param.35) | copy-start | bytes 393220
  486.1 244.5 %copy-start.1 = (f32[8,4096]{1,0:T(8,128)S(1)}, f32[8,4096]{1,0:T(8,128)}, u32[]{:S(2)}) copy-start(f32[8,4096]{1,0:T(8,128)} %reduce-scatter.3.cloned.1.call-done) | copy-start | bytes 393220
  710.8 18.3 %all-to-all-start.1 = ((f32[8,4,4096]{2,1,0:T(4,128)}), f32[8,4,4096]{2,1,0:T(4,128)S(1)}, u32[]{:S(2)}, u32[]{:S(2)}) async-start(f32[8,4,4096]{2,1,0:T(4,128)} %reshape.112), calls=%async_computation.3 | async-start | bytes 1048576 | tf_op jit(solution)/shard_map/all_to_all | solution.py:137
  730.6 0.7 copy-start.3
Sparse Core Ops, SparseCore 0:
  47.7 78.5 all-gather.12
  129.4 75.1 all-gather.10
  207.0 102.1 all-gather.6
  315.4 32.2 reduce-scatter.2
  363.2 97.7 all-gather.8
  486.2 222.6 reduce-scatter.4
where the time goes:
time: 743 us; the launch traced here: 738 us
  waiting for transfers between devices  521 us (70%)
  other arithmetic  103 us (14%)
  blocking collectives  35.9 us (5%)
  matrix products  34.8 us (5%)
  between operations  14.4 us (2%)
  starting transfers between devices  13.2 us (2%)
  local copies, waits for them, and re-layouts  13 us (2%)
    reduce_scatter x1, waiting for transfers between devices, body(): lax.psum_scatter(jnp.dot(activated, down_local, preferred_element_type=jn...  223 us
    all_gather x2, waiting for transfers between devices, entering(): everything = jax.tree.map(lambda part: lax.all_gather(part, axis), array)  155 us
    all_gather x1, waiting for transfers between devices, body(): shard_part = lax.all_gather(arrived, 'seq', axis=0, tiled=True)  97.7 us
    reduce_sum x64, other arithmetic, advance(): return (carried, jnp.sum(output_t[:, None] * carried, axis=0))  61.7 us
    reduce_scatter x1, waiting for transfers between devices, body(): lax.psum_scatter(partial_value, 'exp', scatter_dimension=0, tiled=True)  32 us
    select_n x32, other arithmetic, hop(): return jax.tree.map(lambda a, b: jnp.where(reached, a, b), new, before)  29.3 us
    psum x1, blocking collectives, body(): delta_sum, state_maps = lax.psum((delta_part, state_part), 'exp')  23.9 us
    dot_general x1, matrix products, body(): jnp.dot(activated, down_local, preferred_element_type=jnp.float32)  15.4 us
  transfers between devices with their start and end apart: 8, of which 7 were waited for; matrix products, arithmetic and copies ran while one was open for 14% of the time, Pallas kernels for 0%

commit v1 on v0

--- a/solution.py
+++ b/solution.py
@@ -124,7 +124,15 @@
     gate_local = w_gate[0]
     up_local = w_up[0]
     down_local = w_down[0]
-    shard_part = lax.all_gather(arrived, "seq", axis=0, tiled=True)
+    shard_part = jnp.concatenate(
+        jax.lax.all_to_all(
+            jnp.stack(tuple((arrived for _ in range(jax.lax.psum(1, axis_name="seq"))))),
+            "seq",
+            0,
+            0,
+        ),
+        axis=0,
+    )
     gate_part = jnp.dot(shard_part, gate_local, preferred_element_type=jnp.float32)
     up_part = jnp.dot(shard_part, up_local, preferred_element_type=jnp.float32)
     activated = (jax.nn.silu(gate_part) * up_part).astype(jnp.bfloat16)

time: 743 us -> 837 us (1.13)
  blocking collectives: 35.9 us -> 229 us
  waiting for transfers between devices: 521 us -> 423 us
    all_to_all x0 -> x1, blocking collectives: none -> 193 us  [body(): jax.lax.all_to_all(jnp.stack(tuple((arrived for _ in range(jax.lax.psum(1...]
    all_gather x1 -> x0, waiting for transfers between devices: 97.7 us -> none  [body(): shard_part = lax.all_gather(arrived, 'seq', axis=0, tiled=True)]
  transfers between devices with their start and end apart: 8 -> 7, of which waited for: 7 -> 6; matrix products, arithmetic and copies ran while one was open for 14% -> 12% of each run, Pallas kernels for 0% -> 0%
where the time goes in v1:
time: 837 us; the launch traced here: 832 us
  waiting for transfers between devices  423 us (51%)
  blocking collectives  229 us (27%)
  other arithmetic  103 us (12%)
  matrix products  30.4 us (4%)
  local copies, waits for them, and re-layouts  16.6 us (2%)
  between operations  14.1 us (2%)
  starting transfers between devices  13.1 us (2%)
    reduce_scatter x1, waiting for transfers between devices, body(): lax.psum_scatter(jnp.dot(activated, down_local, preferred_element_type=jn...  223 us
    all_to_all x1, blocking collectives, body(): jax.lax.all_to_all(jnp.stack(tuple((arrived for _ in range(jax.lax.psum(1...  193 us
    all_gather x2, waiting for transfers between devices, entering(): everything = jax.tree.map(lambda part: lax.all_gather(part, axis), array)  155 us
    reduce_sum x64, other arithmetic, advance(): return (carried, jnp.sum(output_t[:, None] * carried, axis=0))  61.7 us
    reduce_scatter x1, waiting for transfers between devices, body(): lax.psum_scatter(partial_value, 'exp', scatter_dimension=0, tiled=True)  31.9 us
    select_n x32, other arithmetic, hop(): return jax.tree.map(lambda a, b: jnp.where(reached, a, b), new, before)  29.3 us
    psum x1, blocking collectives, body(): delta_sum, state_maps = lax.psum((delta_part, state_part), 'exp')  23.9 us
  transfers between devices with their start and end apart: 7, of which 6 were waited for; matrix products, arithmetic and copies ran while one was open for 12% of the time, Pallas kernels for 0%

profile of v1, /device:TPU:1, one launch (start us, length us, event | category | flops | bytes accessed | tf_op | source)
XLA Modules:
  0.0 831.9 jit_solution(14557272979420904484)
XLA Ops:
  8.0 3.9 collective-permute-start
  12.8 1.4 multiply_convert_fusion.1
  14.2 1.2 fusion.34
  15.4 1.0 fusion.35
  16.4 23.9 %all-reduce = (bf16[64,256]{1,0:T(8,128)(2,1)S(1)}, f32[64,32]{0,1:T(8,128)S(1)}) all-reduce(f32[64,256]{1,0:T(8,128)S(1)} %fusion.34, f32[64,32]{0,1:T(8,128)S(1)} %fusion.35), channel_id=1, replica_groups=mesh['seq'=32,'exp'=8] {'exp'}, use_global_device_ids=true, to_apply=%region_0.1 | all-reduce | flops 18432 | bytes 114688 | tf_op jit(solution)/shard_map/psum | solution.py:66
  40.3 1.0 fusion.30
  41.7 1.5 fusion.32
  43.2 4.3 broadcast_multiply_fusion
  49.2 77.0 %all-gather.10.cloned.1.call-done = f32[512,1024]{1,0:T(8,128)} async-done(((f32[16,1024]{1,0:T(8,128)}), f32[512,1024]{1,0:T(8,128)}) %all-gather.10.cloned.1.call-update) | async-done | bytes 2097168 | tf_op jit(solution)/shard_map/all_gather | solution.py:15
  126.2 78.3 %all-gather.8.cloned.1.call-done = f32[512,1024]{1,0:T(8,128)} async-done(((f32[16,1024]{1,0:T(8,128)}), f32[512,1024]{1,0:T(8,128)}) %all-gather.8.cloned.1.call-update) | async-done | bytes 2097168 | tf_op jit(solution)/shard_map/all_gather | solution.py:15
  204.5 30.0 %while.29 = (s32[]{:T(128)}, f32[16,1024]{1,0:T(8,128)S(1)}, s32[]{:T(128)}, f32[32,16,1024]{2,1,0:T(8,128)}, f32[32,16,1024]{2,1,0:T(8,128)}) while((s32[]{:T(128)}, f32[16,1024]{1,0:T(8,128)S(1)}, s32[]{:T(128)}, f32[32,16,1024]{2,1,0:T(8,128)}, f32[32,16,1024]{2,1,0:T(8,128)}) %tuple.89), condition=%wide.region_5.6_spmd.clone.clone, body=%wide.region_4.5_spmd.clone.sunk.clone | while | flops 65540 | bytes 262229 | solution.py:27
  234.5 71.4 %while.28 = (s32[]{:T(128)}, f32[16,1024]{1,0:T(8,128)S(1)}, f32[64,1024]{1,0:T(8,128)S(1)}, f32[64,16,1024]{2,1,0:T(8,128)}, f32[64,16,1024]{2,1,0:T(8,128)}, /*index=5*/f32[64,16]{1,0:T(8,128)S(1)}) while((s32[]{:T(128)}, f32[16,1024]{1,0:T(8,128)S(1)}, f32[64,1024]{1,0:T(8,128)S(1)}, f32[64,16,1024]{2,1,0:T(8,128)}, ...), condition=%wide.region_8.9_spmd.clone, body=%wide.region_6.8_spmd.sunk.clone | while | flops 64514 | bytes 274705 | solution.py:92
  237.9 1.0 multiply_reduce_fusion.6
  241.2 1.0 multiply_reduce_fusion.6
  260.2 1.0 multiply_reduce_fusion.6
  261.3 1.0 multiply_reduce_fusion.6
  262.4 1.0 multiply_reduce_fusion.6
  263.6 1.0 multiply_reduce_fusion.6
  264.7 1.0 multiply_reduce_fusion.6
  270.2 1.0 multiply_reduce_fusion.6
  271.4 1.0 multiply_reduce_fusion.6
  278.1 1.0 multiply_reduce_fusion.6
  279.2 1.0 multiply_reduce_fusion.6
  284.8 1.0 multiply_reduce_fusion.6
  287.0 1.0 multiply_reduce_fusion.6
  288.1 1.0 multiply_reduce_fusion.6
  289.2 1.0 multiply_reduce_fusion.6
  290.4 1.0 multiply_reduce_fusion.6
  291.5 1.0 multiply_reduce_fusion.6
  292.6 1.0 multiply_reduce_fusion.6
  298.2 1.0 multiply_reduce_fusion.6
  299.3 1.0 multiply_reduce_fusion.6
  304.9 1.0 multiply_reduce_fusion.6
  306.0 3.2 all-gather.6.cloned.1.call-done
  309.2 6.1 fusion.20
  315.7 31.9 %reduce-scatter.3.cloned.1.call-done = f32[8,4096]{1,0:T(8,128)} async-done(((f32[64,4096]{1,0:T(8,128)}), f32[8,4096]{1,0:T(8,128)}) %reduce-scatter.3.cloned.1.call-update) | async-done | bytes 131088 | tf_op jit(solution)/shard_map/reduce_scatter | solution.py:101
  347.6 1.1 multiply_reduce_fusion.3
  348.7 1.0 multiply_convert_fusion.2
  350.1 12.0 %all_to_all.30 = bf16[8,4,4096]{2,1,0:T(4,128)(2,1)S(1)} all-to-all(bf16[8,4,4096]{2,1,0:T(4,128)(2,1)S(1)} %all_to_all.19), channel_id=1, replica_groups=mesh['seq'=32,'exp'=8] {'exp'}, dimensions={0} | all-to-all | bytes 524288 | tf_op jit(solution)/shard_map/all_to_all | solution.py:123
  362.2 1.0 stack.5
  363.3 192.7 %all_to_all.31 = bf16[32,32,4096]{2,1,0:T(8,128)(2,1)S(1)} all-to-all(bf16[32,32,4096]{2,1,0:T(8,128)(2,1)S(1)} %stack.5), channel_id=1, replica_groups=mesh['seq'=32,'exp'=8] {'seq'}, dimensions={0} | all-to-all | bytes 16777216 | tf_op jit(solution)/shard_map/all_to_all | solution.py:128
  556.0 3.2 copy-done.2
  559.3 5.2 fusion.5
  564.5 15.5 %convolution_convert_fusion = bf16[1024,4096]{1,0:T(8,128)(2,1)} fusion(bf16[1,448,4096]{2,1,0:T(8,128)(2,1)} %param.38, f32[1024,448]{0,1:T(8,128)} %fusion.5, bf16[1024,4096]{1,0:T(8,128)(2,1)} %bitcast.72, bf16[1,4096,448]{1,2,0:T(8,128)(2,1)} %param.37), kind=kOutput, calls=%fused_computation.9 | convolution fusion | flops 7523139584 | bytes 25952256 | tf_op jit(solution)/shard_map/dot_general | solution.py:140
  580.2 222.7 %reduce-scatter.5.cloned.1.call-done = bf16[32,4096]{1,0:T(8,128)(2,1)} async-done(((bf16[1024,4096]{1,0:T(8,128)(2,1)}), bf16[32,4096]{1,0:T(8,128)(2,1)}) %reduce-scatter.5.cloned.1.call-update) | async-done | bytes 262160 | tf_op jit(solution)/shard_map/reduce_scatter | solution.py:139
  802.9 1.9 reshape.119
  804.8 9.0 %all-to-all-start.2 = ((f32[8,4,4096]{2,1,0:T(4,128)}), f32[8,4,4096]{2,1,0:T(4,128)S(1)}, u32[]{:S(2)}, u32[]{:S(2)}) async-start(f32[8,4,4096]{2,1,0:T(4,128)} %reshape.119), calls=%async_computation.4 | async-start | bytes 1048576 | tf_op jit(solution)/shard_map/all_to_all | solution.py:145
  814.3 9.0 %all-to-all-done.2 = f32[8,4,4096]{2,1,0:T(4,128)S(1)} async-done(((f32[8,4,4096]{2,1,0:T(4,128)}), f32[8,4,4096]{2,1,0:T(4,128)S(1)}, u32[]{:S(2)}, u32[]{:S(2)}) %all-to-all-start.2) | async-done | bytes 524320 | tf_op jit(solution)/shard_map/all_to_all | solution.py:145
  (273 shorter events, 85.7 us)
Async XLA Ops:
  7.2 33.2 %copy-start = (bf16[256,1024]{1,0:T(8,128)(2,1)S(1)}, bf16[256,1024]{1,0:T(8,128)(2,1)}, u32[]{:S(2)}) copy-start(bf16[256,1024]{1,0:T(8,128)(2,1)} %param.28) | copy-start | bytes 1572868
  7.2 119.0 %all-gather.10.cloned.1.call-start = ((), (), s32[]{:S(2)}) async-start(), calls=%async_computation.9 | async-start | bytes 2162688 | tf_op jit(solution)/shard_map/all_gather | solution.py:15
  8.0 4.8 collective-permute-start
  43.2 265.9 %copy-start.6 = (bf16[64,1024]{1,0:T(8,128)(2,1)S(1)}, bf16[64,1024]{1,0:T(8,128)(2,1)}, u32[]{:S(2)}) copy-start(bf16[64,1024]{1,0:T(8,128)(2,1)} %param.23) | copy-start | bytes 393220
  43.2 265.9 %copy-start.8 = (f32[1024]{0:T(1024)S(1)}, f32[1024]{0:T(1024)}, u32[]{:S(2)}) copy-start(f32[1024]{0:T(1024)} %param.31) | copy-start | bytes 12292
  47.6 157.0 %all-gather.8.cloned.1.call-start = ((), (), s32[]{:S(2)}) async-start(), calls=%async_computation.8 | async-start | bytes 2162688 | tf_op jit(solution)/shard_map/all_gather | solution.py:15
  48.3 260.9 %all-gather.6.cloned.1.call-start = ((), (), s32[]{:S(2)}) async-start(), calls=%async_computation.5 | async-start | bytes 8650752 | tf_op jit(solution)/shard_map/all_gather | solution.py:98
  49.0 298.6 %reduce-scatter.3.cloned.1.call-start = ((), (), s32[]{:S(2)}) async-start(), calls=%async_computation.6 | async-start | bytes 1179648 | tf_op jit(solution)/shard_map/reduce_scatter | solution.py:101
  309.2 6.2 copy-start.10
  309.2 38.4 %copy-start.4 = (bf16[8,4096]{1,0:T(8,128)(2,1)S(1)}, bf16[8,4096]{1,0:T(8,128)(2,1)}, u32[]{:S(2)}) copy-start(bf16[8,4096]{1,0:T(8,128)(2,1)} %param.33) | copy-start | bytes 196612
  309.2 39.5 %copy-start.9 = (f32[4096]{0:T(1024)S(1)}, f32[4096]{0:T(1024)}, u32[]{:S(2)}) copy-start(f32[4096]{0:T(1024)} %param.34) | copy-start | bytes 49156
  315.3 487.6 %reduce-scatter.5.cloned.1.call-start = ((), (), s32[]{:S(2)}) async-start(), calls=%async_computation.7 | async-start | bytes 8650752 | tf_op jit(solution)/shard_map/reduce_scatter | solution.py:139
  363.3 196.0 %copy-start.11 = (bf16[1,4096,448]{1,2,0:T(8,128)(2,1)S(1)}, bf16[1,4096,448]{1,2,0:T(8,128)(2,1)}, u32[]{:S(2)}) copy-start(bf16[1,4096,448]{1,2,0:T(8,128)(2,1)} %param.36) | copy-start | bytes 11010052
  556.0 3.2 copy-start.2
  580.0 233.8 %copy-start.7 = (f32[4096,8]{0,1:T(8,128)S(1)}, f32[4096,8]{0,1:T(8,128)}, u32[]{:S(2)}) copy-start(f32[4096,8]{0,1:T(8,128)} %param.35) | copy-start | bytes 393220
  580.0 244.7 %copy-start.3 = (f32[8,4096]{1,0:T(8,128)S(1)}, f32[8,4096]{1,0:T(8,128)}, u32[]{:S(2)}) copy-start(f32[8,4096]{1,0:T(8,128)} %reduce-scatter.3.cloned.1.call-done) | copy-start | bytes 393220
  580.0 245.4 %copy-start.1 = (bf16[256,1024]{1,0:T(8,128)(2,1)S(1)}, bf16[256,1024]{1,0:T(8,128)(2,1)}, u32[]{:S(2)}) copy-start(bf16[256,1024]{1,0:T(8,128)(2,1)} %param.28) | copy-start | bytes 1572868
  804.8 18.5 %all-to-all-start.2 = ((f32[8,4,4096]{2,1,0:T(4,128)}), f32[8,4,4096]{2,1,0:T(4,128)S(1)}, u32[]{:S(2)}, u32[]{:S(2)}) async-start(f32[8,4,4096]{2,1,0:T(4,128)} %reshape.119), calls=%async_computation.4 | async-start | bytes 1048576 | tf_op jit(solution)/shard_map/all_to_all | solution.py:145
  824.7 0.7 copy-start.5
Sparse Core Ops, SparseCore 0:
  47.7 78.4 all-gather.9
  129.4 75.1 all-gather.7
  207.0 102.1 all-gather.5
  315.4 32.1 reduce-scatter.2
  580.1 222.7 reduce-scatter.4
